TPU v7x, 256 devices: a whole 4x4x8 slice. The times are simulated.
256 devices in a mesh: ctx: 32 (over z, y_hi, core), tp: 8 (over x, y_lo).
Axes of the slice: x: 4, y: 4 (y_hi: 2, y_lo: 2; y = y_hi * 2 + y_lo), z: 8, core: 2. Of those that a mesh axis runs over, the one named last changes fastest.
Arguments:
- qkv: bfloat16 [4096, 32, 3, 128], P('ctx', 'tp'), may hold values from -5 to 5
- grad_out: bfloat16 [4096, 8192], P(('ctx', 'tp')), may hold values from -6 to 6
- attn_out: bfloat16 [4096, 8192], P('tp'), may hold values from -0.09375 to 0.09375
Outputs:
- mixed_out: float32 [4096, 8192], P(('ctx', 'tp'))
- grad_qkv: float32 [4096, 32, 3, 128], P('ctx', 'tp')
All inputs are finite; a program needn't handle non-finite values.
Results may differ from a plain program's by a relative error of at most 0.0063.
Values may be sent and summed in bfloat16 or wider, within the bound.
A program may use at most 128 MiB of HBM per device.

v0:
```python
import math

import jax
import jax.numpy as jnp
from jax import lax
from jax.sharding import PartitionSpec as P

HD = 128


def per_device(qkv, grad_out, attn_out):
    row_count, heads_local = (qkv.shape[0], qkv.shape[1])
    factor = 1.0 / math.sqrt(HD)
    queries = qkv[:, :, 0]
    keys_local = qkv[:, :, 1]
    values_local = qkv[:, :, 2]
    all_keys, all_values = (
        lax.all_gather(keys_local, "ctx", axis=0, tiled=True),
        lax.all_gather(values_local, "ctx", axis=0, tiled=True),
    )
    seq_len = all_keys.shape[0]
    offset = lax.axis_index("ctx") * row_count
    query_pos = offset + jnp.arange(row_count, dtype=jnp.int32)
    key_pos = jnp.arange(seq_len, dtype=jnp.int32)
    visible = key_pos[None, :] <= query_pos[:, None]
    scores = (
        jnp.einsum("rhd,shd->hrs", queries, all_keys, preferred_element_type=jnp.float32) * factor
    )
    scores = jnp.where(visible[None], scores, -jnp.inf)
    row_max = jnp.max(scores, axis=2, keepdims=True)
    log_total = row_max + jnp.log(jnp.sum(jnp.exp(scores - row_max), axis=2, keepdims=True))
    weights = jnp.exp(scores - log_total)
    weights_low = weights.astype(jnp.bfloat16)
    attended = jnp.einsum(
        "hrs,shd->rhd", weights_low, all_values, preferred_element_type=jnp.float32
    ).astype(jnp.bfloat16)
    attended_flat = attended.reshape(row_count, heads_local * HD)
    mixed_out = lax.psum_scatter(
        jnp.dot(attended_flat, attn_out, preferred_element_type=jnp.float32),
        "tp",
        scatter_dimension=0,
        tiled=True,
    )
    grad_full = jnp.einsum(
        "nm,km->nk",
        lax.all_gather(grad_out, "tp", axis=0, tiled=True),
        attn_out,
        preferred_element_type=jnp.float32,
    )
    grad_att = grad_full.astype(jnp.bfloat16).reshape(row_count, heads_local, HD)
    row_delta = jnp.einsum("rhd,rhd->rh", grad_att, attended, preferred_element_type=jnp.float32)
    grad_weights = jnp.einsum(
        "rhd,shd->hrs", grad_att, all_values, preferred_element_type=jnp.float32
    )
    grad_scores = (weights * (grad_weights - row_delta.T[:, :, None]) * factor).astype(jnp.bfloat16)
    grad_queries = jnp.einsum(
        "hrs,shd->rhd", grad_scores, all_keys, preferred_element_type=jnp.float32
    )
    grad_k = jnp.einsum("hrs,rhd->shd", grad_scores, queries, preferred_element_type=jnp.float32)
    grad_v = jnp.einsum("hrs,rhd->shd", weights_low, grad_att, preferred_element_type=jnp.float32)
    summed = lax.psum_scatter(
        jnp.concatenate([grad_k, grad_v], axis=2).reshape(row_count * lax.axis_size("ctx"), -1),
        "ctx",
        scatter_dimension=0,
        tiled=True,
    )
    summed = summed.reshape(row_count, heads_local, 2 * HD)
    grad_keys = summed[:, :, :HD]
    grad_vals = summed[:, :, HD:]
    grad_qkv = jnp.stack([grad_queries, grad_keys, grad_vals], axis=2)
    return (mixed_out, grad_qkv)


def solution(mesh):
    in_specs = (P("ctx", "tp", None, None), P(("ctx", "tp"), None), P("tp", None))
    out_specs = (P(("ctx", "tp"), None), P("ctx", "tp", None, None))
    return jax.shard_map(
        per_device, mesh=mesh, in_specs=in_specs, out_specs=out_specs, check_vma=False
    )
```

profile of v0, /device:TPU:1, one launch (start us, length us, event | category | flops | bytes accessed | tf_op | source)
XLA Modules:
  0.0 586.2 jit_solution(18238331224555714299)
XLA Ops:
  7.2 0.0 all-gather.6.cloned.1.call-start
  7.2 0.7 all-gather.6.cloned.1.call-update
  7.9 0.0 all-gather.8.cloned.1.call-start
  7.9 1.2 fusion.16
  9.1 0.7 copy.33
  9.8 0.0 all-gather.8.cloned.1.call-update
  9.8 0.0 all-gather.10.cloned.1.call-start
  9.9 0.8 copy.34
  10.6 0.0 all-gather.10.cloned.1.call-update
  10.7 0.0 reduce-scatter.5.cloned.1.call-start
  10.7 0.4 iota_compare_fusion
  11.1 55.5 %all-gather.6.cloned.1.call-done = bf16[128,8192]{1,0:T(8,128)(2,1)} async-done(((bf16[16,8192]{1,0:T(8,128)(2,1)}), bf16[128,8192]{1,0:T(8,128)(2,1)}) %all-gather.6.cloned.1.call-update) | async-done | bytes 2097168 | tf_op jit(solution)/shard_map/all_gather | solution.py:46
  66.6 6.9 %convolution_convert_fusion = bf16[128,512]{1,0:T(8,128)(2,1)S(1)} fusion(bf16[128,8192]{1,0:T(8,128)(2,1)} %all-gather.6.cloned.1.call-done, bf16[512,8192]{1,0:T(8,128)(2,1)} %param.5), kind=kOutput, calls=%fused_computation.17 | convolution fusion | flops 1073807360 | bytes 10616832 | tf_op jit(solution)/shard_map/nm,km->nk/dot_general | solution.py:44
  73.5 0.1 copy.19
  73.7 84.4 %all-gather.8.cloned.1.call-done = bf16[4096,4,1,128]{3,0,1,2:T(8,128)(2,1)} async-done(((bf16[128,4,1,128]{3,0,1,2:T(8,128)(2,1)}), bf16[4096,4,1,128]{3,0,1,2:T(8,128)(2,1)}) %all-gather.8.cloned.1.call-update) | async-done | bytes 4194320 | tf_op jit(solution)/shard_map/all_gather | solution.py:18
  158.1 3.9 fusion.17
  162.0 0.0 copy-start
  162.0 3.2 copy-done
  165.2 1.3 exponential_reduce_fusion
  166.5 78.5 %all-gather.10.cloned.1.call-done = bf16[4096,4,1,128]{0,3,1,2:T(8,128)(2,1)} async-done(((bf16[128,4,1,128]{0,3,1,2:T(8,128)(2,1)}), bf16[4096,4,1,128]{0,3,1,2:T(8,128)(2,1)}) %all-gather.10.cloned.1.call-update) | async-done | bytes 4194320 | tf_op jit(solution)/shard_map/all_gather | solution.py:19
  245.0 6.0 %fusion.10 = bf16[4,128,128]{1,2,0:T(8,128)(2,1)S(1)} fusion(bf16[4096,4,1,128]{0,3,1,2:T(8,128)(2,1)} %all-gather.10.cloned.1.call-done, f32[4,128,4096]{2,1,0:T(8,128)} %copy-done, f32[4,128]{1,0:T(4,128)S(1)} %log_add_fusion), kind=kOutput, calls=%fused_computation.16 | convolution fusion | flops 541130752 | bytes 12716032 | tf_op jit(solution)/shard_map/hrs,shd->rhd/dot_general | solution.py:34
  251.1 0.1 copy.29
  251.2 0.2 multiply_reduce_fusion
  251.4 0.1 copy.30
  251.5 0.0 copy-start.2
  251.5 4.9 convolution_bitcast_fusion
  256.4 0.0 copy-done.2
  256.4 5.1 multiply_convert_fusion
  261.5 0.0 copy-start.1
  261.5 1.3 convolution_bitcast_fusion.1
  262.8 6.0 %pad_maximum_fusion = f32[4096,4,256]{0,2,1:T(8,128)} fusion(f32[4096,4,128]{0,2,1:T(8,128)S(1)} %convolution_bitcast_fusion, f32[4096,4,128]{0,2,1:T(8,128)S(1)} %convolution_bitcast_fusion.1), kind=kLoop, calls=%fused_computation | loop fusion | flops 4194304 | bytes 33554432 | tf_op jit(solution)/shard_map/concatenate | solution.py:62
  268.8 0.0 copy-done.1
  268.8 0.0 reduce-scatter.5.cloned.1.call-update
  268.8 0.2 reduce-scatter.3.cloned.1.call-start
  269.1 6.7 %fusion.18 = f32[128,8192]{1,0:T(8,128)} fusion(bf16[128,512]{0,1:T(8,128)(2,1)S(1)} %bitcast.50, bf16[512,8192]{1,0:T(8,128)(2,1)} %param.5), kind=kOutput, calls=%fused_computation.26 | convolution fusion | flops 1073741824 | bytes 12713984 | tf_op jit(solution)/shard_map/dot_general | solution.py:39
  275.7 0.0 reduce-scatter.3.cloned.1.call-update
  275.8 5.0 fusion.7
  280.8 200.8 %reduce-scatter.5.cloned.1.call-done = f32[128,1024]{0,1:T(8,128)} async-done(((f32[4096,1024]{0,1:T(8,128)}), f32[128,1024]{0,1:T(8,128)}) %reduce-scatter.5.cloned.1.call-update) | async-done | bytes 524304 | tf_op jit(solution)/shard_map/reduce_scatter | solution.py:61
  481.6 1.1 fusion.15
  482.6 0.1 copy.35
  482.8 0.1 copy.36
  482.9 0.1 pad_maximum_fusion.1
  483.0 1.4 copy.22
  484.3 95.3 %reduce-scatter.3.cloned.1.call-done = f32[16,8192]{1,0:T(8,128)} async-done(((f32[128,8192]{1,0:T(8,128)}), f32[16,8192]{1,0:T(8,128)}) %reduce-scatter.3.cloned.1.call-update) | async-done | bytes 524304 | tf_op jit(solution)/shard_map/reduce_scatter | solution.py:38
  (3 shorter events, 0.0 us)
Async XLA Ops:
  7.2 59.4 %all-gather.6.cloned.1.call-start = ((), (), s32[]{:S(2)}) async-start(), calls=%async_computation.3 | async-start | bytes 2359296 | tf_op jit(solution)/shard_map/all_gather | solution.py:46
  7.9 150.2 %all-gather.8.cloned.1.call-start = ((), (), s32[]{:S(2)}) async-start(), calls=%async_computation.5 | async-start | bytes 4325376 | tf_op jit(solution)/shard_map/all_gather | solution.py:18
  9.8 235.2 %all-gather.10.cloned.1.call-start = ((), (), s32[]{:S(2)}) async-start(), calls=%async_computation.6 | async-start | bytes 4325376 | tf_op jit(solution)/shard_map/all_gather | solution.py:19
  10.7 470.9 %reduce-scatter.5.cloned.1.call-start = ((), (), s32[]{:S(2)}) async-start(), calls=%async_computation.4 | async-start | bytes 17301504 | tf_op jit(solution)/shard_map/reduce_scatter | solution.py:61
  162.0 3.2 copy-start
  251.5 4.9 copy-start.2
  261.5 7.4 %copy-start.1 = (bf16[4,128,4096]{2,1,0:T(8,128)(2,1)}, bf16[4,128,4096]{2,1,0:T(8,128)(2,1)S(1)}, u32[]{:S(2)}) copy-start(bf16[4,128,4096]{2,1,0:T(8,128)(2,1)S(1)} %multiply_convert_fusion) | copy-start | bytes 12582916
  268.8 310.8 %reduce-scatter.3.cloned.1.call-start = ((), (), s32[]{:S(2)}) async-start(), calls=%async_computation.2 | async-start | bytes 4718592 | tf_op jit(solution)/shard_map/reduce_scatter | solution.py:38
Sparse Core Ops, SparseCore 0:
  9.8 56.7 all-gather.5
  70.0 88.1 all-gather.7
  161.3 83.7 all-gather.9
  269.0 212.5 reduce-scatter.4
  484.7 94.9 reduce-scatter.2
where the time goes:
time: 586 us
  waiting for transfers between devices  515 us (88%)
  matrix products  39.8 us (7%)
  between operations  13.9 us (2%)
  local copies, waits for them, and re-layouts  8.93 us (2%)
  other arithmetic  7.96 us (1%)
    reduce_scatter x1, waiting for transfers between devices, per_device(): lax.psum_scatter(jnp.concatenate([grad_k, grad_v], axis=2).reshape(row_co...  201 us
    reduce_scatter x1, waiting for transfers between devices, per_device(): lax.psum_scatter(jnp.dot(attended_flat, attn_out, preferred_element_type=...  95.3 us
    all_gather x1, waiting for transfers between devices, per_device(): lax.all_gather(keys_local, 'ctx', axis=0, tiled=True)  84.4 us
    all_gather x1, waiting for transfers between devices, per_device(): lax.all_gather(values_local, 'ctx', axis=0, tiled=True)  78.5 us
    all_gather x1, waiting for transfers between devices, per_device(): lax.all_gather(grad_out, 'tp', axis=0, tiled=True)  55.5 us
  transfers between devices with their start and end apart: 5, of which 5 were waited for; matrix products, arithmetic and copies ran while one was open for 5% of the time, Pallas kernels for 0%

commit v1 on v0

v1 whole, which is shorter than its diff:
```python
import functools
import math

import jax
import jax.numpy as jnp
from jax import lax
from jax.experimental import pallas as pl
from jax.experimental.pallas import tpu as pltpu
from jax.sharding import PartitionSpec as P

HD = 128
MESH = pl.DeviceIdType.MESH
F32 = jnp.float32
BF16 = jnp.bfloat16
D = 8192
CA = 2048
HALF = D // 2
NT = (((1,), (1,)), ((), ()))
TN = (((0,), (0,)), ((), ()))
NN = (((1,), (0,)), ((), ()))


def dot(a, b, dims):
    return lax.dot_general(a, b, dims, preferred_element_type=F32)


def kernel(
    qkv, go, wo,
    mixed, gqkv,
    w, g, kvb, qb, st, wl, dsb, ot, dqt, gs, gb, asend, ah,
    dkv, sb1, rb1, sb2, rb2, sb3, hb, sbq, hq,
    mf, mb, ra, sa, ra2, rb, sb, rbb,
    lsem, p1s, p1r, p2s, p2r, a1s, a1r, gts, gtr, ats, atr, c1s, c1r, c2s, c2r, c3s, c3r, dqs, dqr,
    mas, mar, ma2s, ma2r, mbs, mbr, mb2s, mb2r,
):
    ctx = lax.axis_index("ctx")
    tp = lax.axis_index("tp")
    h = ctx // 8
    k = ctx % 8
    zb = k // 4
    yh = (k // 2) % 2
    c = k % 2
    x = tp // 2
    yl = tp % 2
    chip = k // 2
    factor = 1.0 / math.sqrt(HD)

    heads_dev = {o: (((h + o) % 4) * 8 + k, tp) for o in (1, 2, 3)}
    core_dev = (ctx + 1 - 2 * c, tp)
    group = [
        (ctx + 4 - 8 * zb, tp),
        (ctx + 2 - 4 * yh, tp),
        (ctx + 6 - 8 * zb - 4 * yh, tp),
    ]
    group_chip = [chip + 2 - 4 * zb, chip + 1 - 2 * yh, 3 - chip]
    x_dev = {d: (ctx, ((x + d) % 4) * 2 + yl) for d in (1, 2, 3)}
    y_dev = (ctx, x * 2 + 1 - yl)

    w_cp = pltpu.make_async_copy(wo, w, lsem.at[0])
    w_cp.start()
    kv_cp = pltpu.make_async_copy(qkv.at[pl.ds(1, 2), h], kvb.at[:, h, k], lsem.at[1])
    kv_cp.start()
    q_cp = pltpu.make_async_copy(qkv.at[0, h], qb.at[h], lsem.at[2])
    q_cp.start()
    g_cp = pltpu.make_async_copy(go, g.at[tp], lsem.at[3])
    g_cp.start()

    barrier = pltpu.get_barrier_semaphore()
    everyone = list(heads_dev.values()) + [core_dev] + group + list(x_dev.values()) + [y_dev]
    for dev in everyone:
        pl.semaphore_signal(barrier, inc=1, device_id=dev, device_id_type=MESH)
    pl.semaphore_wait(barrier, len(everyone))

    sends = []

    def send(src, dst, ssem, rsem, dev):
        cp = pltpu.make_async_remote_copy(
            src_ref=src, dst_ref=dst, send_sem=ssem, recv_sem=rsem, device_id=dev, device_id_type=MESH
        )
        cp.start()
        sends.append(cp)
        return cp

    p1 = {}
    for o in (1, 3, 2):
        hh = (h + o) % 4
        p1[o] = send(
            qkv.at[pl.ds(1, 2), hh], kvb.at[:, h, k], p1s.at[0, o - 1], p1r.at[0, o - 1], heads_dev[o]
        )
    a1 = {}

    def a1_send(i, src, dst, dev):
        a1[i] = send(src, dst, a1s.at[i], a1r.at[i], dev)

    a1_send(0, go, g.at[tp], y_dev)
    a1_send(1, go, g.at[tp], x_dev[1])
    a1_send(2, go, g.at[tp], x_dev[3])
    p1q = {}
    for o in (1, 3, 2):
        hh = (h + o) % 4
        p1q[o] = send(qkv.at[0, hh], qb.at[h], p1s.at[1, o - 1], p1r.at[1, o - 1], heads_dev[o])

    p2 = {}

    def p2_block(o):
        s = (h + 4 - o) % 4
        part = kvb.at[:, s, k]
        for p in range(3):
            p2[p, o] = send(part, part, p2s.at[p, o], p2r.at[p, o], group[p])
        p2[3, o] = send(part, part, p2s.at[3, o], p2r.at[3, o], core_dev)

    def p2_forward(p, o):
        s = (h + 4 - o) % 4
        p2[p, o].wait_recv()
        part = kvb.at[:, s, group_chip[p] * 2 + c]
        p2[4 + p, o] = send(part, part, p2s.at[4 + p, o], p2r.at[4 + p, o], core_dev)

    kv_cp.wait()
    p2_block(0)
    p1[1].wait_recv()
    p2_block(1)
    p1[3].wait_recv()
    p2_block(3)
    a1[0].wait_recv()
    ty = x * 2 + 1 - yl
    a1_send(3, g.at[ty], g.at[ty], x_dev[1])
    a1_send(4, g.at[ty], g.at[ty], x_dev[3])
    p1[2].wait_recv()
    p2_block(2)
    lo = pl.ds(0, HALF)
    hi = pl.ds(HALF, HALF)
    a1[1].wait_recv()
    t_in = ((x + 3) % 4) * 2 + yl
    a1_send(5, g.at[t_in, :, lo], g.at[t_in, :, lo], x_dev[1])
    a1[2].wait_recv()
    t_in = ((x + 1) % 4) * 2 + yl
    a1_send(6, g.at[t_in, :, hi], g.at[t_in, :, hi], x_dev[3])
    for o in (0, 1):
        for p in range(3):
            p2_forward(p, o)
    a1[3].wait_recv()
    t_in = ((x + 3) % 4) * 2 + 1 - yl
    a1_send(7, g.at[t_in, :, lo], g.at[t_in, :, lo], x_dev[1])
    a1[4].wait_recv()
    t_in = ((x + 1) % 4) * 2 + 1 - yl
    a1_send(8, g.at[t_in, :, hi], g.at[t_in, :, hi], x_dev[3])
    for p in range(3):
        p2_forward(p, 3)

    g_cp.wait()
    w_cp.wait()
    for i in (5, 6, 7, 8):
        a1[i].wait_recv()
    gatt = dot(g[...].reshape(HD, D), w[...], NT).astype(BF16)
    for hh in range(4):
        gs[hh] = gatt[:, hh * HD : (hh + 1) * HD]
    gt = {}
    for o in (1, 3, 2):
        gt[o] = send(gs.at[(h + o) % 4], gb.at[h], gts.at[o - 1], gtr.at[o - 1], heads_dev[o])
    gb[h] = gs[h]

    for p in range(3):
        p2_forward(p, 2)
    q_cp.wait()
    for o in (1, 3, 2):
        p1q[o].wait_recv()
    for o in (0, 1, 3, 2):
        for p in (3, 4, 5, 6):
            p2[p, o].wait_recv()

    TK = 256
    col_max = [None] * 4
    for j in range(4):
        rows = 512 - HD * j
        q = qb[pl.ds(j, 4 - j)].reshape(rows, HD)

        def score_tile(kt, m, j=j, rows=rows, q=q):
            keys = kvb[0, j, pl.ds(kt * 2, 2)].reshape(TK, HD)
            s = dot(keys, q, NT) * factor
            key_pos = kt * TK + lax.broadcasted_iota(jnp.int32, (TK, HD), 0)
            row_pos = k * HD + lax.broadcasted_iota(jnp.int32, (TK, HD), 1)
            first = jnp.where(key_pos <= row_pos, s[:, :HD], -jnp.inf)
            s = first if rows == HD else jnp.concatenate([first, s[:, HD:]], axis=1)
            st[j, pl.ds(kt * TK, TK), HD * j :] = s
            return jnp.maximum(m, jnp.max(s, axis=0, keepdims=True))

        m = lax.fori_loop(0, 1024 // TK, score_tile, jnp.full((1, rows), -jnp.inf, F32))
        for s in range(j, 4):
            part = m[:, (s - j) * HD : (s - j + 1) * HD]
            col_max[s] = part if col_max[s] is None else jnp.maximum(col_max[s], part)
    m_all = jnp.concatenate(col_max, axis=1)
    total = [None] * 4
    for j in range(4):
        rows = 512 - HD * j
        mj = m_all[:, HD * j :]

        def exp_tile(kt, acc, j=j, mj=mj):
            p = jnp.exp(st[j, pl.ds(kt * TK, TK), HD * j :] - mj)
            st[j, pl.ds(kt * TK, TK), HD * j :] = p
            return acc + jnp.sum(p, axis=0, keepdims=True)

        acc = lax.fori_loop(0, 1024 // TK, exp_tile, jnp.zeros((1, rows), F32))
        for s in range(j, 4):
            part = acc[:, (s - j) * HD : (s - j + 1) * HD]
            total[s] = part if total[s] is None else total[s] + part
    inv = 1.0 / jnp.concatenate(total, axis=1)
    for j in range(4):
        rows = 512 - HD * j
        inv_j = inv[:, HD * j :]

        def norm_tile(kt, carry, j=j, inv_j=inv_j):
            p = st[j, pl.ds(kt * TK, TK), HD * j :] * inv_j
            st[j, pl.ds(kt * TK, TK), HD * j :] = p
            wl[j, pl.ds(kt * TK, TK), HD * j :] = p.astype(BF16)
            return carry

        lax.fori_loop(0, 1024 // TK, norm_tile, 0)
        vals = kvb[1, j].reshape(1024, HD)
        o_t = dot(vals, wl[j, :, HD * j :], TN)
        if j == 0:
            ot[...] = o_t
        else:
            ot[:, HD * j :] += o_t
    o_low = ot[...].astype(BF16).astype(F32)
    asend[...] = o_low.T.astype(BF16).reshape(4, HD, HD)
    at = {}
    for o in (1, 3, 2):
        at[o] = send(asend.at[(h + o) % 4], ah.at[h], ats.at[o - 1], atr.at[o - 1], heads_dev[o])
    ah[h] = asend[h]

    for o in (1, 3, 2):
        gt[o].wait_recv()
    g_t = gb[...].reshape(512, HD).astype(F32).T
    delta = jnp.sum(g_t * o_low, axis=0, keepdims=True)
    c1 = {}
    c2 = {}
    local_or_remote = []

    def home_send(src, local, remote, ssem, rsem, j):
        @pl.when(h != j)
        def _():
            pltpu.make_async_remote_copy(
                src_ref=src, dst_ref=remote, send_sem=ssem, recv_sem=rsem,
                device_id=(8 * j + k, tp), device_id_type=MESH,
            ).start()

        @pl.when(h == j)
        def _():
            local[...] = src[...]

        local_or_remote.append((src, remote, ssem, rsem, j))

    def backward(j):
        rows = 512 - HD * j
        q = qb[pl.ds(j, 4 - j)].reshape(rows, HD)
        ga = gb[pl.ds(j, 4 - j)].reshape(rows, HD)
        delta_j = delta[:, HD * j :]

        def tile(kt, carry):
            sl = pl.ds(kt * TK, TK)
            vals = kvb[1, j, pl.ds(kt * 2, 2)].reshape(TK, HD)
            dp = dot(vals, ga, NT)
            ds = (st[j, sl, HD * j :] * (dp - delta_j) * factor).astype(BF16)
            dsb[sl, HD * j :] = ds
            dkv[j, 0, pl.ds(kt * 2, 2)] = dot(ds, q, NN).reshape(2, HD, HD)
            dkv[j, 1, pl.ds(kt * 2, 2)] = dot(wl[j, sl, HD * j :], ga, NN).reshape(2, HD, HD)
            return carry

        lax.fori_loop(0, 1024 // TK, tile, 0)
        keys = kvb[0, j].reshape(1024, HD)
        dq_t = dot(keys, dsb[:, HD * j :], TN)
        if j == 0:
            dqt[...] = dq_t
        else:
            dqt[:, HD * j :] += dq_t
        for mm in range(4):
            for kv in range(2):
                sb1[j, mm, kv] = dkv[j, kv, mm * 2 + 1 - c].astype(BF16)
        c1[j] = send(sb1.at[j], rb1.at[j], c1s.at[j], c1r.at[j], core_dev)
        sbq[j] = dqt[:, HD * j : HD * (j + 1)].T.astype(BF16)
        home_send(sbq.at[j], hq.at[h], hq.at[h], dqs.at[j], dqr.at[h], j)

    def chip_sum(j):
        c1[j].wait_recv()
        for p in range(3):
            mp = group_chip[p]
            for kv in range(2):
                sb2[j, p, kv] = (dkv[j, kv, mp * 2 + c] + rb1[j, mp, kv].astype(F32)).astype(BF16)
            c2[j, p] = send(sb2.at[j, p], rb2.at[j, p], c2s.at[j, p], c2r.at[j, p], group[p])

    def finish(j):
        for p in range(3):
            c2[j, p].wait_recv()
        for kv in range(2):
            v = dkv[j, kv, k] + rb1[j, chip, kv].astype(F32)
            for p in range(3):
                v = v + rb2[j, p, kv].astype(F32)
            sb3[j, kv] = v.astype(BF16)
        home_send(sb3.at[j], hb.at[h], hb.at[h], c3s.at[j], c3r.at[h], j)

    backward(0)

    for o in (1, 3, 2):
        at[o].wait_recv()
    att = jnp.concatenate([ah[i] for i in range(4)], axis=1)
    TN_COLS = 1024

    def project(n, carry):
        cols = pl.ds(pl.multiple_of(n * TN_COLS, TN_COLS), TN_COLS)
        r = dot(att, w[:, cols], NN).reshape(4, 2, 16, TN_COLS)
        mf[:, :, :, cols] = r
        mb[:, :, :, cols] = r.astype(BF16)
        return carry

    lax.fori_loop(0, CA // TN_COLS, project, 0)
    ma = send(mb.at[:, 1 - yl, :, pl.ds(0, CA)], ra, mas.at[0], mar.at[0], y_dev)
    lax.fori_loop(CA // TN_COLS, D // TN_COLS, project, 0)
    mbx = {}
    for d in (1, 3, 2):
        mbx[d] = send(
            mb.at[(x + d) % 4, :, :, pl.ds(CA, D - CA)], rb.at[d - 1], mbs.at[d - 1], mbr.at[d - 1], x_dev[d]
        )

    backward(1)
    chip_sum(0)
    backward(2)
    chip_sum(1)
    ma.wait_recv()
    for i in range(4):
        sa[i] = (mf[i, yl, :, :CA] + ra[i].astype(F32)).astype(BF16)
    ma2 = {}
    for d in (1, 3, 2):
        ma2[d] = send(sa.at[(x + d) % 4], ra2.at[d - 1], ma2s.at[d - 1], ma2r.at[d - 1], x_dev[d])
    backward(3)
    chip_sum(2)
    chip_sum(3)
    finish(0)
    finish(1)
    for d in (1, 3, 2):
        mbx[d].wait_recv()

    def sum_b(y):
        v = mf[x, y, :, CA:]
        for d in range(3):
            v = v + rb[d, y].astype(F32)
        return v

    sb[...] = sum_b(1 - yl).astype(BF16)
    mb2 = send(sb, rbb, mb2s.at[0], mb2r.at[0], y_dev)
    finish(2)
    finish(3)
    for d in (1, 3, 2):
        ma2[d].wait_recv()
    v = mf[x, yl, :, :CA] + ra[x].astype(F32)
    for d in range(3):
        v = v + ra2[d].astype(F32)
    mixed[:, :CA] = v
    v = sum_b(yl)
    mb2.wait_recv()
    mixed[:, CA:] = v + rbb[...].astype(F32)

    for o in (1, 2, 3):
        hh = (h + o) % 4
        pltpu.make_async_remote_copy(
            src_ref=sbq.at[0], dst_ref=hq.at[hh], send_sem=dqs.at[0], recv_sem=dqr.at[hh],
            device_id=heads_dev[o], device_id_type=MESH,
        ).wait_recv()
        pltpu.make_async_remote_copy(
            src_ref=sb3.at[0], dst_ref=hb.at[hh], send_sem=c3s.at[0], recv_sem=c3r.at[hh],
            device_id=heads_dev[o], device_id_type=MESH,
        ).wait_recv()
    for i in range(4):
        gqkv[0, i] = hq[i].astype(F32)
        for kv in range(2):
            gqkv[1 + kv, i] = hb[i, kv].astype(F32)

    for cp in sends:
        cp.wait_send()
    for src, remote, ssem, rsem, j in local_or_remote:
        @pl.when(h != j)
        def _(src=src, remote=remote, ssem=ssem, rsem=rsem, j=j):
            pltpu.make_async_remote_copy(
                src_ref=src, dst_ref=remote, send_sem=ssem, recv_sem=rsem,
                device_id=(8 * j + k, tp), device_id_type=MESH,
            ).wait_send()


def per_device(qkv, grad_out, attn_out):
    dma = pltpu.SemaphoreType.DMA
    vm = pltpu.VMEM
    scratch = [
        vm((512, D), BF16),
        vm((8, 16, D), BF16),
        vm((2, 4, 8, HD, HD), BF16),
        vm((4, HD, HD), BF16),
        vm((4, 1024, 512), F32),
        vm((4, 1024, 512), BF16),
        vm((1024, 512), BF16),
        vm((HD, 512), F32),
        vm((HD, 512), F32),
        vm((4, HD, HD), BF16),
        vm((4, HD, HD), BF16),
        vm((4, HD, HD), BF16),
        vm((4, HD, HD), BF16),
        vm((4, 2, 8, HD, HD), F32),
        vm((4, 4, 2, HD, HD), BF16),
        vm((4, 4, 2, HD, HD), BF16),
        vm((4, 3, 2, HD, HD), BF16),
        vm((4, 3, 2, HD, HD), BF16),
        vm((4, 2, HD, HD), BF16),
        vm((4, 2, HD, HD), BF16),
        vm((4, HD, HD), BF16),
        vm((4, HD, HD), BF16),
        vm((4, 2, 16, D), F32),
        vm((4, 2, 16, D), BF16),
        vm((4, 16, CA), BF16),
        vm((4, 16, CA), BF16),
        vm((3, 16, CA), BF16),
        vm((3, 2, 16, D - CA), BF16),
        vm((16, D - CA), BF16),
        vm((16, D - CA), BF16),
        dma((4,)),
        dma((2, 3)), dma((2, 3)),
        dma((7, 4)), dma((7, 4)),
        dma((9,)), dma((9,)),
        dma((3,)), dma((3,)),
        dma((3,)), dma((3,)),
        dma((4,)), dma((4,)),
        dma((4, 3)), dma((4, 3)),
        dma((4,)), dma((4,)),
        dma((4,)), dma((4,)),
        dma((1,)), dma((1,)),
        dma((3,)), dma((3,)),
        dma((3,)), dma((3,)),
        dma((1,)), dma((1,)),
    ]
    qkv_t = qkv.transpose(2, 1, 0, 3)
    mixed, gq = pl.pallas_call(
        kernel,
        out_shape=(
            jax.ShapeDtypeStruct((16, D), F32),
            jax.ShapeDtypeStruct((3, 4, HD, HD), F32),
        ),
        in_specs=[pl.BlockSpec(memory_space=pl.ANY)] * 3,
        out_specs=(pl.BlockSpec(memory_space=pltpu.VMEM), pl.BlockSpec(memory_space=pltpu.VMEM)),
        scratch_shapes=scratch,
        compiler_params=pltpu.CompilerParams(
            collective_id=0, has_side_effects=True, vmem_limit_bytes=60 * 1024 * 1024
        ),
    )(qkv_t, grad_out, attn_out)
    return mixed, gq.transpose(2, 1, 0, 3)


def solution(mesh):
    in_specs = (P("ctx", "tp", None, None), P(("ctx", "tp"), None), P("tp", None))
    out_specs = (P(("ctx", "tp"), None), P("ctx", "tp", None, None))
    return jax.shard_map(
        per_device, mesh=mesh, in_specs=in_specs, out_specs=out_specs, check_vma=False
    )
```

time: 586 us -> 85.3 us (0.15)
  waiting for transfers between devices: 515 us -> 0 us
  Pallas kernels: 0 us -> 78.2 us
  matrix products: 39.8 us -> 0 us
  between operations: 13.9 us -> 0.64 us
  other arithmetic: 7.96 us -> 0 us
    reduce_scatter x2 -> x0, waiting for transfers between devices: 296 us -> none  [the longest x1 201 us: per_device(): lax.psum_scatter(jnp.concatenate([grad_k, grad_v], axis=2).reshape(row_co...]
    all_gather x3 -> x0, waiting for transfers between devices: 218 us -> none  [the longest x1 84.4 us: per_device(): lax.all_gather(keys_local, 'ctx', axis=0, tiled=True)]
    pallas_call x0 -> x1, Pallas kernels: none -> 78.2 us  [per_device(): pl.pallas_call(kernel, out_shape=(jax.ShapeDtypeStruct((16, D), F32), jax...]
    dot_general x8 -> x0, matrix products: 39.8 us -> none  [the longest x1 6.94 us: per_device(): jnp.einsum('nm,km->nk', lax.all_gather(grad_out, 'tp', axis=0, tiled=True...]
    concatenate x1 -> x0, other arithmetic: 6.04 us -> none  [per_device(): jnp.concatenate([grad_k, grad_v], axis=2)]
  transfers between devices with their start and end apart: 5 -> 0, of which waited for: 5 -> 0; matrix products, arithmetic and copies ran while one was open for 5% -> 0% of each run, Pallas kernels for 0% -> 0%
where the time goes in v1:
time: 85.3 us; the launch traced here: 85.1 us
  Pallas kernels  78.2 us (92%)
  local copies, waits for them, and re-layouts  6.2 us (7%)
    pallas_call x1, Pallas kernels, per_device(): pl.pallas_call(kernel, out_shape=(jax.ShapeDtypeStruct((16, D), F32), jax...  78.2 us
    unnamed x3, local copies, waits for them, and re-layouts  6.2 us

profile of v1, /device:TPU:1, one launch (start us, length us, event | category | flops | bytes accessed | tf_op | source)
XLA Modules:
  0.0 85.1 jit_solution(12251184066649984167)
XLA Ops:
  0.6 1.8 %copy.8 = bf16[128,4,3,128]{3,0,1,2:T(8,128)(2,1)} copy(bf16[128,4,3,128]{3,1,2,0:T(4,128)(2,1)} %param.3) | data formatting | bytes 786432 | tf_op args[0]
  2.4 78.2 %shard_map.50 = (f32[16,8192]{1,0:T(8,128)}, f32[3,4,128,128]{3,2,1,0:T(8,128)}) custom-call(bf16[3,4,128,128]{3,2,1,0:T(8,128)(2,1)} %bitcast.4, bf16[16,8192]{1,0:T(8,128)(2,1)} %go.1, bf16[512,8192]{1,0:T(8,128)(2,1)} %wo.1), custom_call_target="tpu_custom_call" | custom-call | tf_op jit(solution)/shard_map/pallas_call | solution.py:438
  80.7 2.5 %copy.6 = f32[128,4,3,128]{3,1,2,0:T(4,128)} copy(f32[128,4,3,128]{3,0,1,2:T(8,128)} %bitcast.5) | data formatting | bytes 1572864
  83.2 1.9 %copy.10 = f32[16,8192]{1,0:T(8,128)} copy(f32[16,8192]{1,0:T(8,128)} %get-tuple-element.10) | data formatting | bytes 1048576

commit v2 on v1

v2 whole, which is shorter than its diff:
```python
import functools
import math

import jax
import jax.numpy as jnp
from jax import lax
from jax.experimental import pallas as pl
from jax.experimental.pallas import tpu as pltpu
from jax.sharding import PartitionSpec as P

HD = 128
MESH = pl.DeviceIdType.MESH
F32 = jnp.float32
BF16 = jnp.bfloat16
D = 8192
HALF = D // 2
PIECES = 4
PC = D // PIECES
PH = PC // 2
NT = (((1,), (1,)), ((), ()))
TN = (((0,), (0,)), ((), ()))
NN = (((1,), (0,)), ((), ()))


def dot(a, b, dims):
    return lax.dot_general(a, b, dims, preferred_element_type=F32)


def kernel(
    qkv, go, wo,
    mixed, dq_out, dkv_out,
    raw, wide, qkvt, w, g, kvb, qb, st, wl, dsb, ot, dqt, gs, gb, asend, ah,
    dkv, sb1, rb1, sb2, rb2, sb3, hb, sbq, hq,
    mf, mb, r1l, r1h, accl, acch, rx, sy, ry, mo,
    lsem, ssem, p1r, p2r, p2c, a1r, gtr, atr, c1r, c2r, c3r, dqr, mr, osem,
):
    ctx = lax.axis_index("ctx")
    tp = lax.axis_index("tp")
    h = ctx // 8
    k = ctx % 8
    zb = k // 4
    yh = (k // 2) % 2
    c = k % 2
    x = tp // 2
    yl = tp % 2
    chip = k // 2
    factor = 1.0 / math.sqrt(HD)

    heads_dev = {o: (((h + o) % 4) * 8 + k, tp) for o in (1, 2, 3)}
    core_dev = (ctx + 1 - 2 * c, tp)
    group = [
        (ctx + 4 - 8 * zb, tp),
        (ctx + 2 - 4 * yh, tp),
        (ctx + 6 - 8 * zb - 4 * yh, tp),
    ]
    group_chip = [chip + 2 - 4 * zb, chip + 1 - 2 * yh, 3 - chip]
    x_dev = {d: (ctx, ((x + d) % 4) * 2 + yl) for d in (1, 2, 3)}
    y_dev = (ctx, x * 2 + 1 - yl)

    raw_cp = pltpu.make_async_copy(qkv, raw, lsem.at[1])
    raw_cp.start()
    g_cp = pltpu.make_async_copy(go, g.at[tp], lsem.at[2])
    g_cp.start()
    w_cp = pltpu.make_async_copy(wo, w, lsem.at[0])
    w_cp.start()

    everyone = list(heads_dev.values()) + [core_dev] + group + list(x_dev.values()) + [y_dev]
    barrier = pltpu.get_barrier_semaphore()
    for dev in everyone:
        pl.semaphore_signal(barrier, inc=1, device_id=dev, device_id_type=MESH)
    raw_cp.wait()
    wide[...] = raw[...].astype(F32)
    for kind in (1, 0, 2):
        for hh in range(4):
            qkvt[kind, hh] = wide[pl.ds(kind * 4 + hh, HD, stride=12), :].astype(BF16)
    for kind in range(2):
        kvb[kind, h, k] = qkvt[1 + kind, h]
    qb[h] = qkvt[0, h]
    pl.semaphore_wait(barrier, len(everyone))

    def send(src, dst, rsem, dev):
        cp = pltpu.make_async_remote_copy(
            src_ref=src, dst_ref=dst, send_sem=ssem.at[0], recv_sem=rsem, device_id=dev, device_id_type=MESH
        )
        cp.start()
        return cp

    def received(ref, rsem):
        pltpu.make_async_remote_copy(
            src_ref=ref, dst_ref=ref, send_sem=ssem.at[0], recv_sem=rsem, device_id=core_dev, device_id_type=MESH
        ).wait_recv()

    def p1_send(kind, dst, o, sem):
        return send(qkvt.at[kind, (h + o) % 4], dst, p1r.at[sem], heads_dev[o])

    p2 = {}

    def p2_send(kv, role, o, member, dev):
        part = kvb.at[kv, (h + 4 - o) % 4, member]
        if dev is core_dev:
            send(part, part, p2c.at[kv], dev)
        else:
            p2[kv, role, o] = send(part, part, p2r.at[kv, role, o], dev)

    def p2_own(kv, o):
        p2_send(kv, 0, o, k, group[0])
        p2_send(kv, 1, o, k, group[1])
        p2_send(kv, 2, o, k, core_dev)

    def p2_forward(kv, o):
        first = 1 - kv
        for side in (first, 1 - first):
            p2[kv, side, o].wait_recv()
            member = group_chip[side] * 2 + c
            if side == first:
                p2_send(kv, 2, o, member, group[1 - first])
            p2_send(kv, 3, o, member, core_dev)

    def p2_last(kv, o):
        p2[kv, 2, o].wait_recv()
        p2_send(kv, 3, o, group_chip[2] * 2 + c, core_dev)

    def p2_wait(kv):
        received(kvb.at[kv, :, pl.ds(0, 4)], p2c.at[kv])

    a1 = {}

    def a1_send(i, src, dst, dev):
        a1[i] = send(src, dst, a1r.at[min(i, 5)], dev)

    lo = pl.ds(0, HALF)
    hi = pl.ds(HALF, HALF)
    ty = x * 2 + 1 - yl

    def a1_forward(i, first, other):
        a1[first].wait_recv()
        t = ((x + 3) % 4) * 2 + other
        a1_send(i, g.at[t, :, lo], g.at[t, :, lo], x_dev[1])
        a1[first + 1].wait_recv()
        t = ((x + 1) % 4) * 2 + other
        a1_send(i + 1, g.at[t, :, hi], g.at[t, :, hi], x_dev[3])

    p1k = {}
    for o in (1, 3, 2):
        p1k[o] = p1_send(1, kvb.at[0, h, k], o, o - 1)
    p2_own(0, 0)
    a1_send(0, go, g.at[tp], y_dev)
    a1_send(1, go, g.at[tp], x_dev[1])
    a1_send(2, go, g.at[tp], x_dev[3])
    for o in (1, 3):
        p1k[o].wait_recv()
        p2_own(0, o)
    p1v = {}
    for o in (1, 3, 2):
        p1v[o] = p1_send(2, kvb.at[1, h, k], o, 2 + o)
    for o in (1, 3, 2):
        p1_send(0, qb.at[h], o, 6)
    p1k[2].wait_recv()
    p2_own(0, 2)
    p2_own(1, 0)
    a1[0].wait_recv()
    a1_send(3, g.at[ty], g.at[ty], x_dev[1])
    a1_send(4, g.at[ty], g.at[ty], x_dev[3])
    a1_forward(5, 1, yl)
    p2_forward(0, 0)
    p2_forward(0, 1)
    for o in (1, 3, 2):
        p1v[o].wait_recv()
        p2_own(1, o)
    p2_forward(0, 3)
    p2_forward(0, 2)
    p2_forward(1, 0)
    a1_forward(7, 3, 1 - yl)
    for o in (0, 1, 3, 2):
        p2_last(0, o)
    for o in (1, 3, 2):
        p2_forward(1, o)
    received(qb.at[pl.ds(0, 3)], p1r.at[6])
    p2_wait(0)

    TK = 256
    col_max = [None] * 4
    for j in range(4):
        rows = 512 - HD * j
        q = qb[pl.ds(j, 4 - j)].reshape(rows, HD)

        def score_tile(kt, m, j=j, rows=rows, q=q):
            keys = kvb[0, j, pl.ds(kt * 2, 2)].reshape(TK, HD)
            s = dot(keys, q, NT) * factor
            key_pos = kt * TK + lax.broadcasted_iota(jnp.int32, (TK, HD), 0)
            row_pos = k * HD + lax.broadcasted_iota(jnp.int32, (TK, HD), 1)
            first = jnp.where(key_pos <= row_pos, s[:, :HD], -jnp.inf)
            s = first if rows == HD else jnp.concatenate([first, s[:, HD:]], axis=1)
            st[j, pl.ds(kt * TK, TK), HD * j :] = s
            return jnp.maximum(m, jnp.max(s, axis=0, keepdims=True))

        m = lax.fori_loop(0, 1024 // TK, score_tile, jnp.full((1, rows), -jnp.inf, F32))
        for s in range(j, 4):
            part = m[:, (s - j) * HD : (s - j + 1) * HD]
            col_max[s] = part if col_max[s] is None else jnp.maximum(col_max[s], part)
    g_cp.wait()
    w_cp.wait()
    received(g.at[pl.ds(0, 2)], a1r.at[5])
    gatt = dot(g[...].reshape(HD, D), w[...], NT).astype(BF16)
    for hh in range(4):
        gs[hh] = gatt[:, hh * HD : (hh + 1) * HD]
    for o in (1, 3, 2):
        send(gs.at[(h + o) % 4], gb.at[h], gtr.at[0], heads_dev[o])
    gb[h] = gs[h]
    for o in (0, 1, 3, 2):
        p2_last(1, o)
    m_all = jnp.concatenate(col_max, axis=1)
    total = [None] * 4
    for j in range(4):
        rows = 512 - HD * j
        mj = m_all[:, HD * j :]

        def exp_tile(kt, acc, j=j, mj=mj):
            p = jnp.exp(st[j, pl.ds(kt * TK, TK), HD * j :] - mj)
            st[j, pl.ds(kt * TK, TK), HD * j :] = p
            return acc + jnp.sum(p, axis=0, keepdims=True)

        acc = lax.fori_loop(0, 1024 // TK, exp_tile, jnp.zeros((1, rows), F32))
        for s in range(j, 4):
            part = acc[:, (s - j) * HD : (s - j + 1) * HD]
            total[s] = part if total[s] is None else total[s] + part
    p2_wait(1)
    inv = 1.0 / jnp.concatenate(total, axis=1)
    for j in range(4):
        rows = 512 - HD * j
        inv_j = inv[:, HD * j :]

        def norm_tile(kt, carry, j=j, inv_j=inv_j):
            p = st[j, pl.ds(kt * TK, TK), HD * j :] * inv_j
            st[j, pl.ds(kt * TK, TK), HD * j :] = p
            wl[j, pl.ds(kt * TK, TK), HD * j :] = p.astype(BF16)
            return carry

        lax.fori_loop(0, 1024 // TK, norm_tile, 0)
        vals = kvb[1, j].reshape(1024, HD)
        o_t = dot(vals, wl[j, :, HD * j :], TN)
        if j == 0:
            ot[...] = o_t
        else:
            ot[:, HD * j :] += o_t
    o_low = ot[...].astype(BF16).astype(F32)
    asend[...] = o_low.T.astype(BF16).reshape(4, HD, HD)
    for o in (1, 3, 2):
        send(asend.at[(h + o) % 4], ah.at[h], atr.at[0], heads_dev[o])
    ah[h] = asend[h]

    received(gs.at[pl.ds(0, 3)], gtr.at[0])
    g_t = gb[...].reshape(512, HD).astype(F32).T
    delta = jnp.sum(g_t * o_low, axis=0, keepdims=True)
    c1 = {}

    def home_send(src, local, rsem, j):
        @pl.when(h != j)
        def _():
            send(src, local, rsem, (8 * j + k, tp))

        @pl.when(h == j)
        def _():
            local[...] = src[...]

    def backward(j):
        rows = 512 - HD * j
        q = qb[pl.ds(j, 4 - j)].reshape(rows, HD)
        ga = gb[pl.ds(j, 4 - j)].reshape(rows, HD)
        delta_j = delta[:, HD * j :]

        def tile(kt, carry):
            sl = pl.ds(kt * TK, TK)
            vals = kvb[1, j, pl.ds(kt * 2, 2)].reshape(TK, HD)
            dp = dot(vals, ga, NT)
            ds = (st[j, sl, HD * j :] * (dp - delta_j) * factor).astype(BF16)
            dsb[sl, HD * j :] = ds
            dkv[j, 0, pl.ds(kt * 2, 2)] = dot(ds, q, NN).reshape(2, HD, HD)
            dkv[j, 1, pl.ds(kt * 2, 2)] = dot(wl[j, sl, HD * j :], ga, NN).reshape(2, HD, HD)
            return carry

        lax.fori_loop(0, 1024 // TK, tile, 0)
        keys = kvb[0, j].reshape(1024, HD)
        dq_t = dot(keys, dsb[:, HD * j :], TN)
        if j == 0:
            dqt[...] = dq_t
        else:
            dqt[:, HD * j :] += dq_t
        for mm in range(4):
            for kv in range(2):
                sb1[j, mm, kv] = dkv[j, kv, mm * 2 + 1 - c].astype(BF16)
        c1[j] = send(sb1.at[j], rb1.at[j], c1r.at[j], core_dev)
        sbq[j] = dqt[:, HD * j : HD * (j + 1)].T.astype(BF16)
        home_send(sbq.at[j], hq.at[h], dqr.at[0], j)

    def chip_sum(j):
        c1[j].wait_recv()
        for p in range(3):
            mp = group_chip[p]
            for kv in range(2):
                sb2[j, p, kv] = (dkv[j, kv, mp * 2 + c] + rb1[j, mp, kv].astype(F32)).astype(BF16)
            send(sb2.at[j, p], rb2.at[j, p], c2r.at[j], group[p])

    def finish(j):
        received(rb2.at[j], c2r.at[j])
        for kv in range(2):
            v = dkv[j, kv, k] + rb1[j, chip, kv].astype(F32)
            for p in range(3):
                v = v + rb2[j, p, kv].astype(F32)
            sb3[j, kv] = v.astype(BF16)
        home_send(sb3.at[j], hb.at[h], c3r.at[0], j)

    backward(0)
    backward(1)
    chip_sum(0)

    received(asend.at[pl.ds(0, 3)], atr.at[0])
    att = jnp.concatenate([ah[i] for i in range(4)], axis=1)
    m_cp = {}
    xr, xo, xl = (x + 1) % 4, (x + 2) % 4, (x + 3) % 4

    def m_send(n, i, src, dst, dev):
        m_cp[n, i] = send(src, dst, mr.at[n, i], dev)

    def project(n):
        for half in range(2):
            cols = pl.ds(n * PC + half * PH, PH)
            r = dot(att, w[:, cols], NN).reshape(4, 2, 16, PH)
            mf[:, :, :, cols] = r
            mb[:, :, :, cols] = r.astype(BF16)
        left = pl.ds(n * PC, PH)
        right = pl.ds(n * PC + PH, PH)
        m_send(n, 0, mb.at[xo, :, :, left], r1l.at[n], x_dev[1])
        m_send(n, 1, mb.at[xo, :, :, right], r1h.at[n], x_dev[3])
        m_send(n, 2, mb.at[xr, :, :, right], rx.at[n, 0, :, :, pl.ds(PH, PH)], x_dev[1])
        m_send(n, 2, mb.at[xl, :, :, left], rx.at[n, 1, :, :, pl.ds(0, PH)], x_dev[3])

    def pass_on(n):
        m_cp[n, 0].wait_recv()
        accl[n] = (mf[xr, :, :, pl.ds(n * PC, PH)] + r1l[n].astype(F32)).astype(BF16)
        m_send(n, 2, accl.at[n], rx.at[n, 0, :, :, pl.ds(0, PH)], x_dev[1])
        m_cp[n, 1].wait_recv()
        acch[n] = (mf[xl, :, :, pl.ds(n * PC + PH, PH)] + r1h[n].astype(F32)).astype(BF16)
        m_send(n, 2, acch.at[n], rx.at[n, 1, :, :, pl.ds(PH, PH)], x_dev[3])

    def x_total(n, y):
        return mf[x, y, :, pl.ds(n * PC, PC)] + rx[n, 0, y].astype(F32) + rx[n, 1, y].astype(F32)

    def over_y(n):
        received(rx.at[n], mr.at[n, 2])
        sy[n] = x_total(n, 1 - yl).astype(BF16)
        m_send(n, 3, sy.at[n], ry.at[n], y_dev)

    def out(src, dst, i):
        pltpu.make_async_copy(src, dst, osem.at[i]).start()

    def last_sum(n):
        v = x_total(n, yl)
        m_cp[n, 3].wait_recv()
        cols = pl.ds(n * PC, PC)
        mo[:, cols] = v + ry[n].astype(F32)
        out(mo.at[:, cols], mixed.at[:, cols], 0)

    for n in range(PIECES):
        project(n)
    backward(2)
    chip_sum(1)
    pass_on(0)
    backward(3)
    chip_sum(2)
    pass_on(1)
    chip_sum(3)
    finish(0)
    pass_on(2)
    finish(1)
    pass_on(3)
    over_y(0)
    finish(2)
    over_y(1)
    finish(3)
    over_y(2)
    over_y(3)
    for n in range(PIECES):
        last_sum(n)

    received(sbq.at[pl.ds(0, 3)], dqr.at[0])
    out(hq, dq_out, 1)
    received(sb3.at[pl.ds(0, 3)], c3r.at[0])
    out(hb, dkv_out, 2)

    everything = w.at[pl.ds(0, 496)]
    pltpu.make_async_remote_copy(
        src_ref=everything, dst_ref=everything, send_sem=ssem.at[0], recv_sem=p1r.at[0],
        device_id=core_dev, device_id_type=MESH,
    ).wait_send()
    pltpu.make_async_copy(mo, mixed, osem.at[0]).wait()
    pltpu.make_async_copy(hq, dq_out, osem.at[1]).wait()
    pltpu.make_async_copy(hb, dkv_out, osem.at[2]).wait()


def finish_kernel(mixed_in, dq, dkv, mixed, rows_out, rows, sem):
    copies = [pltpu.make_async_copy(mixed_in, mixed, sem.at[0])]
    copies[0].start()
    n = 32
    for part in range(HD // n):
        pos = pl.ds(part * n, n)
        for i in range(4):
            for kind in range(3):
                v = dq[i, pos] if kind == 0 else dkv[i, kind - 1, pos]
                rows[pl.ds(part * n * 12 + kind * 4 + i, n, stride=12), :] = v.astype(F32)
        span = pl.ds(part * n * 12, n * 12)
        copies.append(pltpu.make_async_copy(rows.at[span], rows_out.at[span], sem.at[1 + part]))
        copies[-1].start()
    for cp in copies:
        cp.wait()


def per_device(qkv, grad_out, attn_out):
    dma = pltpu.SemaphoreType.DMA
    vm = pltpu.VMEM
    scratch = [
        vm((1536, HD), BF16),
        vm((1536, HD), F32),
        vm((3, 4, HD, HD), BF16),
        vm((512, D), BF16),
        vm((8, 16, D), BF16),
        vm((2, 4, 8, HD, HD), BF16),
        vm((4, HD, HD), BF16),
        vm((4, 1024, 512), F32),
        vm((4, 1024, 512), BF16),
        vm((1024, 512), BF16),
        vm((HD, 512), F32),
        vm((HD, 512), F32),
        vm((4, HD, HD), BF16),
        vm((4, HD, HD), BF16),
        vm((4, HD, HD), BF16),
        vm((4, HD, HD), BF16),
        vm((4, 2, 8, HD, HD), F32),
        vm((4, 4, 2, HD, HD), BF16),
        vm((4, 4, 2, HD, HD), BF16),
        vm((4, 3, 2, HD, HD), BF16),
        vm((4, 3, 2, HD, HD), BF16),
        vm((4, 2, HD, HD), BF16),
        vm((4, 2, HD, HD), BF16),
        vm((4, HD, HD), BF16),
        vm((4, HD, HD), BF16),
        vm((4, 2, 16, D), F32),
        vm((4, 2, 16, D), BF16),
        vm((PIECES, 2, 16, PH), BF16),
        vm((PIECES, 2, 16, PH), BF16),
        vm((PIECES, 2, 16, PH), BF16),
        vm((PIECES, 2, 16, PH), BF16),
        vm((PIECES, 2, 2, 16, PC), BF16),
        vm((PIECES, 16, PC), BF16),
        vm((PIECES, 16, PC), BF16),
        vm((16, D), F32),
        dma((3,)),
        dma((1,)),
        dma((7,)),
        dma((2, 3, 4)), dma((2,)),
        dma((6,)),
        dma((1,)), dma((1,)),
        dma((4,)), dma((4,)),
        dma((1,)), dma((1,)),
        dma((PIECES, 4)),
        dma((3,)),
    ]
    rows = qkv.transpose(0, 2, 1, 3).reshape(1536, HD)
    mixed, dq, dkv = pl.pallas_call(
        kernel,
        out_shape=(
            jax.ShapeDtypeStruct((16, D), F32),
            jax.ShapeDtypeStruct((4, HD, HD), BF16),
            jax.ShapeDtypeStruct((4, 2, HD, HD), BF16),
        ),
        in_specs=[pl.BlockSpec(memory_space=pl.ANY)] * 3,
        out_specs=[pl.BlockSpec(memory_space=pl.ANY)] * 3,
        scratch_shapes=scratch,
        compiler_params=pltpu.CompilerParams(
            collective_id=0, has_side_effects=True, vmem_limit_bytes=60 * 1024 * 1024
        ),
    )(rows, grad_out, attn_out)
    mixed, grads = pl.pallas_call(
        finish_kernel,
        out_shape=(
            jax.ShapeDtypeStruct((16, D), F32),
            jax.ShapeDtypeStruct((1536, HD), F32),
        ),
        in_specs=[pl.BlockSpec(memory_space=pltpu.VMEM)] * 3,
        out_specs=[pl.BlockSpec(memory_space=pl.ANY)] * 2,
        scratch_shapes=[pltpu.VMEM((1536, HD), F32), pltpu.SemaphoreType.DMA((5,))],
    )(mixed, dq, dkv)
    return mixed, grads.reshape(HD, 3, 4, HD).transpose(0, 2, 1, 3)


def solution(mesh):
    in_specs = (P("ctx", "tp", None, None), P(("ctx", "tp"), None), P("tp", None))
    out_specs = (P(("ctx", "tp"), None), P("ctx", "tp", None, None))
    return jax.shard_map(
        per_device, mesh=mesh, in_specs=in_specs, out_specs=out_specs, check_vma=False
    )
```

time: 85.3 us -> 73.2 us (0.86)
  local copies, waits for them, and re-layouts: 6.2 us -> 0 us
  Pallas kernels: 78.2 us -> 72.5 us
    pallas_call x1, Pallas kernels: 78.2 us -> 70.2 us  [per_device(): pl.pallas_call(kernel, out_shape=(jax.ShapeDtypeStruct((16, D), F32), jax...]
    unnamed x3 -> x0, local copies, waits for them, and re-layouts: 6.2 us -> none
    pallas_call x0 -> x1, Pallas kernels: none -> 2.26 us  [per_device(): pl.pallas_call(finish_kernel, out_shape=(jax.ShapeDtypeStruct((16, D), F3...]
where the time goes in v2:
time: 73.2 us; the launch traced here: 73.1 us
  Pallas kernels  72.5 us (99%)
    pallas_call x1, Pallas kernels, per_device(): pl.pallas_call(kernel, out_shape=(jax.ShapeDtypeStruct((16, D), F32), jax...  70.2 us
    pallas_call x1, Pallas kernels, per_device(): pl.pallas_call(finish_kernel, out_shape=(jax.ShapeDtypeStruct((16, D), F3...  2.26 us

profile of v2, /device:TPU:1, one launch (start us, length us, event | category | flops | bytes accessed | tf_op | source)
XLA Modules:
  0.0 73.1 jit_solution(2709457818195681950)
XLA Ops:
  0.6 70.2 %shard_map.50 = (f32[16,8192]{1,0:T(8,128)}, bf16[4,128,128]{2,1,0:T(8,128)(2,1)}, bf16[4,2,128,128]{3,2,1,0:T(8,128)(2,1)}) custom-call(bf16[1536,128]{1,0:T(8,128)(2,1)} %bitcast.6, bf16[16,8192]{1,0:T(8,128)(2,1)} %go.1, bf16[512,8192]{1,0:T(8,128)(2,1)} %wo.1), custom_call_target="tpu_custom_call" | custom-call | tf_op jit(solution)/shard_map/pallas_call | solution.py:469
  70.8 2.3 %shard_map.51 = (f32[16,8192]{1,0:T(8,128)}, f32[1536,128]{1,0:T(8,128)}) custom-call(f32[16,8192]{1,0:T(8,128)} %get-tuple-element.7.mixed_in, bf16[4,128,128]{2,1,0:T(8,128)(2,1)} %get-tuple-element.8.dq, bf16[4,2,128,128]{3,2,1,0:T(8,128)(2,1)} %get-tuple-element.9.dkv), custom_call_target="tpu_custom_call" | custom-call | tf_op jit(solution)/shard_map/pallas_call | solution.py:483

commit v3 on v2

--- a/solution.py
+++ b/solution.py
@@ -30,8 +30,8 @@
     qkv, go, wo,
     mixed, dq_out, dkv_out,
     raw, wide, qkvt, w, g, kvb, qb, st, wl, dsb, ot, dqt, gs, gb, asend, ah,
-    dkv, sb1, rb1, sb2, rb2, sb3, hb, sbq, hq,
-    mf, mb, r1l, r1h, accl, acch, rx, sy, ry, mo,
+    dkv, sb1, rb1, s2a, r2a, s2b, r2b, sb3, hb, sbq, hq,
+    mf, mb, r1l, r1h, accl, acch, rx, sy, ry, ra, sa, r1a, acca, rxa, mo,
     lsem, ssem, p1r, p2r, p2c, a1r, gtr, atr, c1r, c2r, c3r, dqr, mr, osem,
 ):
     ctx = lax.axis_index("ctx")
@@ -108,7 +108,7 @@
         p2_send(kv, 2, o, k, core_dev)
 
     def p2_forward(kv, o):
-        first = 1 - kv
+        first = 1 if kv == 0 and o < 2 else 0
         for side in (first, 1 - first):
             p2[kv, side, o].wait_recv()
             member = group_chip[side] * 2 + c
@@ -123,54 +123,56 @@
     def p2_wait(kv):
         received(kvb.at[kv, :, pl.ds(0, 4)], p2c.at[kv])
 
-    a1 = {}
-
-    def a1_send(i, src, dst, dev):
-        a1[i] = send(src, dst, a1r.at[min(i, 5)], dev)
-
     lo = pl.ds(0, HALF)
     hi = pl.ds(HALF, HALF)
     ty = x * 2 + 1 - yl
 
-    def a1_forward(i, first, other):
-        a1[first].wait_recv()
+    def a1_send(src, t, half, sem, dev):
+        return send(src.at[:, half], g.at[t, :, half], a1r.at[sem], dev)
+
+    def a1_forward(i, other):
+        received(g.at[0, :, lo], a1r.at[i])
         t = ((x + 3) % 4) * 2 + other
-        a1_send(i, g.at[t, :, lo], g.at[t, :, lo], x_dev[1])
-        a1[first + 1].wait_recv()
+        a1_send(g.at[t], t, lo, 6, x_dev[1])
+        received(g.at[0, :, hi], a1r.at[i + 1])
         t = ((x + 1) % 4) * 2 + other
-        a1_send(i + 1, g.at[t, :, hi], g.at[t, :, hi], x_dev[3])
+        a1_send(g.at[t], t, hi, 6, x_dev[3])
 
     p1k = {}
     for o in (1, 3, 2):
         p1k[o] = p1_send(1, kvb.at[0, h, k], o, o - 1)
+    a1_send(go, tp, lo, 2, x_dev[1])
+    a1_send(go, tp, hi, 3, x_dev[3])
+    a1_send(go, tp, lo, 0, y_dev)
+    a1_send(go, tp, hi, 1, y_dev)
+    a1_send(go, tp, hi, 6, x_dev[1])
+    a1_send(go, tp, lo, 6, x_dev[3])
     p2_own(0, 0)
-    a1_send(0, go, g.at[tp], y_dev)
-    a1_send(1, go, g.at[tp], x_dev[1])
-    a1_send(2, go, g.at[tp], x_dev[3])
     for o in (1, 3):
         p1k[o].wait_recv()
         p2_own(0, o)
     p1v = {}
     for o in (1, 3, 2):
         p1v[o] = p1_send(2, kvb.at[1, h, k], o, 2 + o)
-    for o in (1, 3, 2):
-        p1_send(0, qb.at[h], o, 6)
+    a1_forward(2, yl)
+    received(g.at[0, :, lo], a1r.at[0])
+    a1_send(g.at[ty], ty, lo, 4, x_dev[1])
     p1k[2].wait_recv()
     p2_own(0, 2)
+    for o in (1, 3, 2):
+        p1_send(0, qb.at[h], o, 6)
+    received(g.at[0, :, hi], a1r.at[1])
+    a1_send(g.at[ty], ty, hi, 5, x_dev[3])
+    a1_send(g.at[ty], ty, hi, 6, x_dev[1])
+    a1_send(g.at[ty], ty, lo, 6, x_dev[3])
+    for o in (0, 1, 3, 2):
+        p2_forward(0, o)
     p2_own(1, 0)
-    a1[0].wait_recv()
-    a1_send(3, g.at[ty], g.at[ty], x_dev[1])
-    a1_send(4, g.at[ty], g.at[ty], x_dev[3])
-    a1_forward(5, 1, yl)
-    p2_forward(0, 0)
-    p2_forward(0, 1)
     for o in (1, 3, 2):
         p1v[o].wait_recv()
         p2_own(1, o)
-    p2_forward(0, 3)
-    p2_forward(0, 2)
+    a1_forward(4, 1 - yl)
     p2_forward(1, 0)
-    a1_forward(7, 3, 1 - yl)
     for o in (0, 1, 3, 2):
         p2_last(0, o)
     for o in (1, 3, 2):
@@ -178,67 +180,48 @@
     received(qb.at[pl.ds(0, 3)], p1r.at[6])
     p2_wait(0)
 
-    TK = 256
     col_max = [None] * 4
+    key_pos = lax.broadcasted_iota(jnp.int32, (1024, HD), 0)
+    row_pos = k * HD + lax.broadcasted_iota(jnp.int32, (1024, HD), 1)
     for j in range(4):
         rows = 512 - HD * j
-        q = qb[pl.ds(j, 4 - j)].reshape(rows, HD)
-
-        def score_tile(kt, m, j=j, rows=rows, q=q):
-            keys = kvb[0, j, pl.ds(kt * 2, 2)].reshape(TK, HD)
-            s = dot(keys, q, NT) * factor
-            key_pos = kt * TK + lax.broadcasted_iota(jnp.int32, (TK, HD), 0)
-            row_pos = k * HD + lax.broadcasted_iota(jnp.int32, (TK, HD), 1)
-            first = jnp.where(key_pos <= row_pos, s[:, :HD], -jnp.inf)
-            s = first if rows == HD else jnp.concatenate([first, s[:, HD:]], axis=1)
-            st[j, pl.ds(kt * TK, TK), HD * j :] = s
-            return jnp.maximum(m, jnp.max(s, axis=0, keepdims=True))
-
-        m = lax.fori_loop(0, 1024 // TK, score_tile, jnp.full((1, rows), -jnp.inf, F32))
-        for s in range(j, 4):
-            part = m[:, (s - j) * HD : (s - j + 1) * HD]
-            col_max[s] = part if col_max[s] is None else jnp.maximum(col_max[s], part)
-    g_cp.wait()
-    w_cp.wait()
-    received(g.at[pl.ds(0, 2)], a1r.at[5])
-    gatt = dot(g[...].reshape(HD, D), w[...], NT).astype(BF16)
-    for hh in range(4):
-        gs[hh] = gatt[:, hh * HD : (hh + 1) * HD]
-    for o in (1, 3, 2):
-        send(gs.at[(h + o) % 4], gb.at[h], gtr.at[0], heads_dev[o])
-    gb[h] = gs[h]
-    for o in (0, 1, 3, 2):
-        p2_last(1, o)
+        s = dot(kvb[0, j].reshape(1024, HD), qb[pl.ds(j, 4 - j)].reshape(rows, HD), NT) * factor
+        first = jnp.where(key_pos <= row_pos, s[:, :HD], -jnp.inf)
+        s = first if rows == HD else jnp.concatenate([first, s[:, HD:]], axis=1)
+        st[j, :, HD * j :] = s
+        m = jnp.max(s, axis=0, keepdims=True)
+        for i in range(j, 4):
+            part = m[:, (i - j) * HD : (i - j + 1) * HD]
+            col_max[i] = part if col_max[i] is None else jnp.maximum(col_max[i], part)
     m_all = jnp.concatenate(col_max, axis=1)
     total = [None] * 4
     for j in range(4):
-        rows = 512 - HD * j
-        mj = m_all[:, HD * j :]
-
-        def exp_tile(kt, acc, j=j, mj=mj):
-            p = jnp.exp(st[j, pl.ds(kt * TK, TK), HD * j :] - mj)
-            st[j, pl.ds(kt * TK, TK), HD * j :] = p
-            return acc + jnp.sum(p, axis=0, keepdims=True)
-
-        acc = lax.fori_loop(0, 1024 // TK, exp_tile, jnp.zeros((1, rows), F32))
-        for s in range(j, 4):
-            part = acc[:, (s - j) * HD : (s - j + 1) * HD]
-            total[s] = part if total[s] is None else total[s] + part
+        p = jnp.exp(st[j, :, HD * j :] - m_all[:, HD * j :])
+        st[j, :, HD * j :] = p
+        m = jnp.sum(p, axis=0, keepdims=True)
+        for i in range(j, 4):
+            part = m[:, (i - j) * HD : (i - j + 1) * HD]
+            total[i] = part if total[i] is None else total[i] + part
+    inv = 1.0 / jnp.concatenate(total, axis=1)
+    g_cp.wait()
+    w_cp.wait()
+    received(g.at[pl.ds(0, 4)], a1r.at[6])
+    gatt = dot(g[:, :, :HALF].reshape(HD, HALF), w[:, :HALF], NT)
+    for o in (0, 1, 3, 2):
+        p2_last(1, o)
+    gatt = (gatt + dot(g[:, :, HALF:].reshape(HD, HALF), w[:, HALF:], NT)).astype(BF16)
+    for hh in range(4):
+        gs[hh] = gatt[:, hh * HD : (hh + 1) * HD]
+    for o in (1, 3, 2):
+        send(gs.at[(h + o) % 4], gb.at[h], gtr.at[0], heads_dev[o])
+    gb[h] = gs[h]
     p2_wait(1)
-    inv = 1.0 / jnp.concatenate(total, axis=1)
     for j in range(4):
-        rows = 512 - HD * j
-        inv_j = inv[:, HD * j :]
-
-        def norm_tile(kt, carry, j=j, inv_j=inv_j):
-            p = st[j, pl.ds(kt * TK, TK), HD * j :] * inv_j
-            st[j, pl.ds(kt * TK, TK), HD * j :] = p
-            wl[j, pl.ds(kt * TK, TK), HD * j :] = p.astype(BF16)
-            return carry
-
-        lax.fori_loop(0, 1024 // TK, norm_tile, 0)
-        vals = kvb[1, j].reshape(1024, HD)
-        o_t = dot(vals, wl[j, :, HD * j :], TN)
+        p = st[j, :, HD * j :] * inv[:, HD * j :]
+        st[j, :, HD * j :] = p
+        p_low = p.astype(BF16)
+        wl[j, :, HD * j :] = p_low
+        o_t = dot(kvb[1, j].reshape(1024, HD), p_low, TN)
         if j == 0:
             ot[...] = o_t
         else:
@@ -249,9 +232,6 @@
         send(asend.at[(h + o) % 4], ah.at[h], atr.at[0], heads_dev[o])
     ah[h] = asend[h]
 
-    received(gs.at[pl.ds(0, 3)], gtr.at[0])
-    g_t = gb[...].reshape(512, HD).astype(F32).T
-    delta = jnp.sum(g_t * o_low, axis=0, keepdims=True)
     c1 = {}
 
     def home_send(src, local, rsem, j):
@@ -269,17 +249,11 @@
         ga = gb[pl.ds(j, 4 - j)].reshape(rows, HD)
         delta_j = delta[:, HD * j :]
 
-        def tile(kt, carry):
-            sl = pl.ds(kt * TK, TK)
-            vals = kvb[1, j, pl.ds(kt * 2, 2)].reshape(TK, HD)
-            dp = dot(vals, ga, NT)
-            ds = (st[j, sl, HD * j :] * (dp - delta_j) * factor).astype(BF16)
-            dsb[sl, HD * j :] = ds
-            dkv[j, 0, pl.ds(kt * 2, 2)] = dot(ds, q, NN).reshape(2, HD, HD)
-            dkv[j, 1, pl.ds(kt * 2, 2)] = dot(wl[j, sl, HD * j :], ga, NN).reshape(2, HD, HD)
-            return carry
-
-        lax.fori_loop(0, 1024 // TK, tile, 0)
+        dp = dot(kvb[1, j].reshape(1024, HD), ga, NT)
+        ds = (st[j, :, HD * j :] * (dp - delta_j) * factor).astype(BF16)
+        dsb[:, HD * j :] = ds
+        dkv[j, 0] = dot(ds, q, NN).reshape(8, HD, HD)
+        dkv[j, 1] = dot(wl[j, :, HD * j :], ga, NN).reshape(8, HD, HD)
         keys = kvb[0, j].reshape(1024, HD)
         dq_t = dot(keys, dsb[:, HD * j :], TN)
         if j == 0:
@@ -293,29 +267,29 @@
         sbq[j] = dqt[:, HD * j : HD * (j + 1)].T.astype(BF16)
         home_send(sbq.at[j], hq.at[h], dqr.at[0], j)
 
+    def of_chip(j, kv, mp):
+        return dkv[j, kv, mp * 2 + c] + rb1[j, mp, kv].astype(F32)
+
     def chip_sum(j):
         c1[j].wait_recv()
-        for p in range(3):
-            mp = group_chip[p]
-            for kv in range(2):
-                sb2[j, p, kv] = (dkv[j, kv, mp * 2 + c] + rb1[j, mp, kv].astype(F32)).astype(BF16)
-            send(sb2.at[j, p], rb2.at[j, p], c2r.at[j], group[p])
+        for kv in range(2):
+            s2a[j, kv, 0] = of_chip(j, kv, group_chip[kv]).astype(BF16)
+            s2a[j, kv, 1] = of_chip(j, kv, group_chip[2]).astype(BF16)
+            send(s2a.at[j, kv], r2a.at[j, kv], c2r.at[0, j], group[kv])
+
+    def relay(j):
+        received(r2a.at[j], c2r.at[0, j])
+        for kv in range(2):
+            s2b[j, kv] = (of_chip(j, kv, group_chip[1 - kv]) + r2a[j, kv, 1].astype(F32)).astype(BF16)
+            send(s2b.at[j, kv], r2b.at[j, kv], c2r.at[1, j], group[1 - kv])
 
     def finish(j):
-        received(rb2.at[j], c2r.at[j])
+        received(r2b.at[j], c2r.at[1, j])
         for kv in range(2):
-            v = dkv[j, kv, k] + rb1[j, chip, kv].astype(F32)
-            for p in range(3):
-                v = v + rb2[j, p, kv].astype(F32)
+            v = of_chip(j, kv, chip) + r2a[j, kv, 0].astype(F32) + r2b[j, kv].astype(F32)
             sb3[j, kv] = v.astype(BF16)
         home_send(sb3.at[j], hb.at[h], c3r.at[0], j)
 
-    backward(0)
-    backward(1)
-    chip_sum(0)
-
-    received(asend.at[pl.ds(0, 3)], atr.at[0])
-    att = jnp.concatenate([ah[i] for i in range(4)], axis=1)
     m_cp = {}
     xr, xo, xl = (x + 1) % 4, (x + 2) % 4, (x + 3) % 4
 
@@ -328,10 +302,16 @@
             r = dot(att, w[:, cols], NN).reshape(4, 2, 16, PH)
             mf[:, :, :, cols] = r
             mb[:, :, :, cols] = r.astype(BF16)
+
+    def first_hop(n):
         left = pl.ds(n * PC, PH)
         right = pl.ds(n * PC + PH, PH)
         m_send(n, 0, mb.at[xo, :, :, left], r1l.at[n], x_dev[1])
         m_send(n, 1, mb.at[xo, :, :, right], r1h.at[n], x_dev[3])
+
+    def direct(n):
+        left = pl.ds(n * PC, PH)
+        right = pl.ds(n * PC + PH, PH)
         m_send(n, 2, mb.at[xr, :, :, right], rx.at[n, 0, :, :, pl.ds(PH, PH)], x_dev[1])
         m_send(n, 2, mb.at[xl, :, :, left], rx.at[n, 1, :, :, pl.ds(0, PH)], x_dev[3])
 
@@ -343,6 +323,36 @@
         acch[n] = (mf[xl, :, :, pl.ds(n * PC + PH, PH)] + r1h[n].astype(F32)).astype(BF16)
         m_send(n, 2, acch.at[n], rx.at[n, 1, :, :, pl.ds(PH, PH)], x_dev[3])
 
+    last = PIECES - 1
+    cols_a = pl.ds(last * PC, PC)
+
+    def a_over_y():
+        m_send(last, 3, mb.at[:, 1 - yl, :, cols_a], ra, y_dev)
+
+    def a_first_hop():
+        m_cp[last, 3].wait_recv()
+        for i in range(4):
+            v = mf[i, yl, :, cols_a] + ra[i].astype(F32)
+            mf[i, yl, :, cols_a] = v
+            sa[i] = v.astype(BF16)
+        m_send(last, 0, sa.at[xo, :, pl.ds(0, PH)], r1a.at[0], x_dev[1])
+        m_send(last, 1, sa.at[xo, :, pl.ds(PH, PH)], r1a.at[1], x_dev[3])
+        m_send(last, 2, sa.at[xr, :, pl.ds(PH, PH)], rxa.at[0, :, pl.ds(PH, PH)], x_dev[1])
+        m_send(last, 2, sa.at[xl, :, pl.ds(0, PH)], rxa.at[1, :, pl.ds(0, PH)], x_dev[3])
+
+    def a_pass_on():
+        m_cp[last, 0].wait_recv()
+        acca[0] = (mf[xr, yl, :, pl.ds(last * PC, PH)] + r1a[0].astype(F32)).astype(BF16)
+        m_send(last, 2, acca.at[0], rxa.at[0, :, pl.ds(0, PH)], x_dev[1])
+        m_cp[last, 1].wait_recv()
+        acca[1] = (mf[xl, yl, :, pl.ds(last * PC + PH, PH)] + r1a[1].astype(F32)).astype(BF16)
+        m_send(last, 2, acca.at[1], rxa.at[1, :, pl.ds(PH, PH)], x_dev[3])
+
+    def a_last_sum():
+        received(rxa, mr.at[last, 2])
+        mo[:, cols_a] = mf[x, yl, :, cols_a] + rxa[0].astype(F32) + rxa[1].astype(F32)
+        out(mo.at[:, cols_a], mixed.at[:, cols_a], 0)
+
     def x_total(n, y):
         return mf[x, y, :, pl.ds(n * PC, PC)] + rx[n, 0, y].astype(F32) + rx[n, 1, y].astype(F32)
 
@@ -361,28 +371,46 @@
         mo[:, cols] = v + ry[n].astype(F32)
         out(mo.at[:, cols], mixed.at[:, cols], 0)
 
-    for n in range(PIECES):
+    received(gs.at[pl.ds(0, 3)], gtr.at[0])
+    g_t = gb[...].reshape(512, HD).astype(F32).T
+    delta = jnp.sum(g_t * o_low, axis=0, keepdims=True)
+    backward(0)
+    received(asend.at[pl.ds(0, 3)], atr.at[0])
+    att = jnp.concatenate([ah[i] for i in range(4)], axis=1)
+    project(last)
+    a_over_y()
+    for n in range(last):
         project(n)
+        first_hop(n)
+    direct(0)
+    direct(1)
+    backward(1)
+    chip_sum(0)
+    pass_on(0)
+    direct(2)
     backward(2)
     chip_sum(1)
-    pass_on(0)
+    pass_on(1)
     backward(3)
     chip_sum(2)
-    pass_on(1)
+    relay(0)
+    pass_on(2)
     chip_sum(3)
+    relay(1)
+    a_first_hop()
+    relay(2)
+    over_y(0)
+    relay(3)
     finish(0)
-    pass_on(2)
+    a_pass_on()
     finish(1)
-    pass_on(3)
-    over_y(0)
+    over_y(1)
     finish(2)
-    over_y(1)
     finish(3)
     over_y(2)
-    over_y(3)
-    for n in range(PIECES):
+    for n in range(last):
         last_sum(n)
-
+    a_last_sum()
     received(sbq.at[pl.ds(0, 3)], dqr.at[0])
     out(hq, dq_out, 1)
     received(sb3.at[pl.ds(0, 3)], c3r.at[0])
@@ -438,29 +466,36 @@
         vm((4, 2, 8, HD, HD), F32),
         vm((4, 4, 2, HD, HD), BF16),
         vm((4, 4, 2, HD, HD), BF16),
-        vm((4, 3, 2, HD, HD), BF16),
-        vm((4, 3, 2, HD, HD), BF16),
+        vm((4, 2, 2, HD, HD), BF16),
+        vm((4, 2, 2, HD, HD), BF16),
         vm((4, 2, HD, HD), BF16),
         vm((4, 2, HD, HD), BF16),
+        vm((4, 2, HD, HD), BF16),
+        vm((4, 2, HD, HD), BF16),
         vm((4, HD, HD), BF16),
         vm((4, HD, HD), BF16),
         vm((4, 2, 16, D), F32),
         vm((4, 2, 16, D), BF16),
-        vm((PIECES, 2, 16, PH), BF16),
-        vm((PIECES, 2, 16, PH), BF16),
-        vm((PIECES, 2, 16, PH), BF16),
-        vm((PIECES, 2, 16, PH), BF16),
-        vm((PIECES, 2, 2, 16, PC), BF16),
-        vm((PIECES, 16, PC), BF16),
-        vm((PIECES, 16, PC), BF16),
+        vm((PIECES - 1, 2, 16, PH), BF16),
+        vm((PIECES - 1, 2, 16, PH), BF16),
+        vm((PIECES - 1, 2, 16, PH), BF16),
+        vm((PIECES - 1, 2, 16, PH), BF16),
+        vm((PIECES - 1, 2, 2, 16, PC), BF16),
+        vm((PIECES - 1, 16, PC), BF16),
+        vm((PIECES - 1, 16, PC), BF16),
+        vm((4, 16, PC), BF16),
+        vm((4, 16, PC), BF16),
+        vm((2, 16, PH), BF16),
+        vm((2, 16, PH), BF16),
+        vm((2, 16, PC), BF16),
         vm((16, D), F32),
         dma((3,)),
         dma((1,)),
         dma((7,)),
         dma((2, 3, 4)), dma((2,)),
-        dma((6,)),
+        dma((7,)),
         dma((1,)), dma((1,)),
-        dma((4,)), dma((4,)),
+        dma((4,)), dma((2, 4)),
         dma((1,)), dma((1,)),
         dma((PIECES, 4)),
         dma((3,)),

time: 73.2 us -> 70.6 us (0.964); the launches traced: 73.1 us -> 69.6 us
  Pallas kernels: 72.5 us -> 68.9 us
    pallas_call x1, Pallas kernels: 70.2 us -> 66.7 us  [per_device(): pl.pallas_call(kernel, out_shape=(jax.ShapeDtypeStruct((16, D), F32), jax...]
where the time goes in v3:
time: 70.6 us; the launch traced here: 69.6 us
  Pallas kernels  68.9 us (98%)
    pallas_call x1, Pallas kernels, per_device(): pl.pallas_call(kernel, out_shape=(jax.ShapeDtypeStruct((16, D), F32), jax...  66.7 us
    pallas_call x1, Pallas kernels, per_device(): pl.pallas_call(finish_kernel, out_shape=(jax.ShapeDtypeStruct((16, D), F3...  2.26 us

profile of v3, /device:TPU:1, one launch (start us, length us, event | category | flops | bytes accessed | tf_op | source)
XLA Modules:
  0.0 69.6 jit_solution(1339579761597333823)
XLA Ops:
  0.6 66.7 %shard_map.50 = (f32[16,8192]{1,0:T(8,128)}, bf16[4,128,128]{2,1,0:T(8,128)(2,1)}, bf16[4,2,128,128]{3,2,1,0:T(8,128)(2,1)}) custom-call(bf16[1536,128]{1,0:T(8,128)(2,1)} %bitcast.6, bf16[16,8192]{1,0:T(8,128)(2,1)} %go.1, bf16[512,8192]{1,0:T(8,128)(2,1)} %wo.1), custom_call_target="tpu_custom_call" | custom-call | tf_op jit(solution)/shard_map/pallas_call | solution.py:504
  67.3 2.3 %shard_map.51 = (f32[16,8192]{1,0:T(8,128)}, f32[1536,128]{1,0:T(8,128)}) custom-call(f32[16,8192]{1,0:T(8,128)} %get-tuple-element.7.mixed_in, bf16[4,128,128]{2,1,0:T(8,128)(2,1)} %get-tuple-element.8.dq, bf16[4,2,128,128]{3,2,1,0:T(8,128)(2,1)} %get-tuple-element.9.dkv), custom_call_target="tpu_custom_call" | custom-call | tf_op jit(solution)/shard_map/pallas_call | solution.py:518

commit v4 on v3

--- a/solution.py
+++ b/solution.py
@@ -203,18 +203,8 @@
             part = m[:, (i - j) * HD : (i - j + 1) * HD]
             total[i] = part if total[i] is None else total[i] + part
     inv = 1.0 / jnp.concatenate(total, axis=1)
-    g_cp.wait()
-    w_cp.wait()
-    received(g.at[pl.ds(0, 4)], a1r.at[6])
-    gatt = dot(g[:, :, :HALF].reshape(HD, HALF), w[:, :HALF], NT)
     for o in (0, 1, 3, 2):
         p2_last(1, o)
-    gatt = (gatt + dot(g[:, :, HALF:].reshape(HD, HALF), w[:, HALF:], NT)).astype(BF16)
-    for hh in range(4):
-        gs[hh] = gatt[:, hh * HD : (hh + 1) * HD]
-    for o in (1, 3, 2):
-        send(gs.at[(h + o) % 4], gb.at[h], gtr.at[0], heads_dev[o])
-    gb[h] = gs[h]
     p2_wait(1)
     for j in range(4):
         p = st[j, :, HD * j :] * inv[:, HD * j :]
@@ -231,6 +221,16 @@
     for o in (1, 3, 2):
         send(asend.at[(h + o) % 4], ah.at[h], atr.at[0], heads_dev[o])
     ah[h] = asend[h]
+
+    g_cp.wait()
+    w_cp.wait()
+    received(g.at[pl.ds(0, 4)], a1r.at[6])
+    gatt = dot(g[...].reshape(HD, D), w[...], NT).astype(BF16)
+    for hh in range(4):
+        gs[hh] = gatt[:, hh * HD : (hh + 1) * HD]
+    for o in (1, 3, 2):
+        send(gs.at[(h + o) % 4], gb.at[h], gtr.at[0], heads_dev[o])
+    gb[h] = gs[h]
 
     c1 = {}
 
@@ -371,10 +371,6 @@
         mo[:, cols] = v + ry[n].astype(F32)
         out(mo.at[:, cols], mixed.at[:, cols], 0)
 
-    received(gs.at[pl.ds(0, 3)], gtr.at[0])
-    g_t = gb[...].reshape(512, HD).astype(F32).T
-    delta = jnp.sum(g_t * o_low, axis=0, keepdims=True)
-    backward(0)
     received(asend.at[pl.ds(0, 3)], atr.at[0])
     att = jnp.concatenate([ah[i] for i in range(4)], axis=1)
     project(last)
@@ -384,30 +380,34 @@
         first_hop(n)
     direct(0)
     direct(1)
+    received(gs.at[pl.ds(0, 3)], gtr.at[0])
+    g_t = gb[...].reshape(512, HD).astype(F32).T
+    delta = jnp.sum(g_t * o_low, axis=0, keepdims=True)
+    backward(0)
     backward(1)
     chip_sum(0)
+    backward(2)
+    chip_sum(1)
+    backward(3)
     pass_on(0)
     direct(2)
-    backward(2)
-    chip_sum(1)
+    chip_sum(2)
     pass_on(1)
-    backward(3)
-    chip_sum(2)
+    chip_sum(3)
+    pass_on(2)
     relay(0)
-    pass_on(2)
-    chip_sum(3)
+    a_first_hop()
     relay(1)
-    a_first_hop()
+    over_y(0)
     relay(2)
-    over_y(0)
     relay(3)
     finish(0)
     a_pass_on()
     finish(1)
     over_y(1)
     finish(2)
+    over_y(2)
     finish(3)
-    over_y(2)
     for n in range(last):
         last_sum(n)
     a_last_sum()

time: 70.6 us -> 67.4 us (0.955); the launches traced: 69.6 us -> 67.3 us
  Pallas kernels: 68.9 us -> 66.6 us
    pallas_call x1, Pallas kernels: 66.7 us -> 64.4 us  [per_device(): pl.pallas_call(kernel, out_shape=(jax.ShapeDtypeStruct((16, D), F32), jax...]
where the time goes in v4:
time: 67.4 us; the launch traced here: 67.3 us
  Pallas kernels  66.6 us (99%)
    pallas_call x1, Pallas kernels, per_device(): pl.pallas_call(kernel, out_shape=(jax.ShapeDtypeStruct((16, D), F32), jax...  64.4 us
    pallas_call x1, Pallas kernels, per_device(): pl.pallas_call(finish_kernel, out_shape=(jax.ShapeDtypeStruct((16, D), F3...  2.26 us

profile of v4, /device:TPU:1, one launch (start us, length us, event | category | flops | bytes accessed | tf_op | source)
XLA Modules:
  0.0 67.3 jit_solution(13666090302179357749)
XLA Ops:
  0.6 64.4 %shard_map.50 = (f32[16,8192]{1,0:T(8,128)}, bf16[4,128,128]{2,1,0:T(8,128)(2,1)}, bf16[4,2,128,128]{3,2,1,0:T(8,128)(2,1)}) custom-call(bf16[1536,128]{1,0:T(8,128)(2,1)} %bitcast.6, bf16[16,8192]{1,0:T(8,128)(2,1)} %go.1, bf16[512,8192]{1,0:T(8,128)(2,1)} %wo.1), custom_call_target="tpu_custom_call" | custom-call | tf_op jit(solution)/shard_map/pallas_call | solution.py:504
  65.0 2.3 %shard_map.51 = (f32[16,8192]{1,0:T(8,128)}, f32[1536,128]{1,0:T(8,128)}) custom-call(f32[16,8192]{1,0:T(8,128)} %get-tuple-element.7.mixed_in, bf16[4,128,128]{2,1,0:T(8,128)(2,1)} %get-tuple-element.8.dq, bf16[4,2,128,128]{3,2,1,0:T(8,128)(2,1)} %get-tuple-element.9.dkv), custom_call_target="tpu_custom_call" | custom-call | tf_op jit(solution)/shard_map/pallas_call | solution.py:518

commit v5 on v4

--- a/solution.py
+++ b/solution.py
@@ -31,7 +31,7 @@
     mixed, dq_out, dkv_out,
     raw, wide, qkvt, w, g, kvb, qb, st, wl, dsb, ot, dqt, gs, gb, asend, ah,
     dkv, sb1, rb1, s2a, r2a, s2b, r2b, sb3, hb, sbq, hq,
-    mf, mb, r1l, r1h, accl, acch, rx, sy, ry, ra, sa, r1a, acca, rxa, mo,
+    mf, mb, r1l, r1h, accl, acch, rx, sy, ry, ra, sa, r1a, acca, rxa, mo, gacc,
     lsem, ssem, p1r, p2r, p2c, a1r, gtr, atr, c1r, c2r, c3r, dqr, mr, osem,
 ):
     ctx = lax.axis_index("ctx")
@@ -205,6 +205,10 @@
     inv = 1.0 / jnp.concatenate(total, axis=1)
     for o in (0, 1, 3, 2):
         p2_last(1, o)
+    g_cp.wait()
+    w_cp.wait()
+    received(g.at[pl.ds(0, 4)], a1r.at[6])
+    gacc[...] = dot(g[:, :, :HALF].reshape(HD, HALF), w[:, :HALF], NT)
     p2_wait(1)
     for j in range(4):
         p = st[j, :, HD * j :] * inv[:, HD * j :]
@@ -222,10 +226,7 @@
         send(asend.at[(h + o) % 4], ah.at[h], atr.at[0], heads_dev[o])
     ah[h] = asend[h]
 
-    g_cp.wait()
-    w_cp.wait()
-    received(g.at[pl.ds(0, 4)], a1r.at[6])
-    gatt = dot(g[...].reshape(HD, D), w[...], NT).astype(BF16)
+    gatt = (gacc[...] + dot(g[:, :, HALF:].reshape(HD, HALF), w[:, HALF:], NT)).astype(BF16)
     for hh in range(4):
         gs[hh] = gatt[:, hh * HD : (hh + 1) * HD]
     for o in (1, 3, 2):
@@ -395,8 +396,8 @@
     pass_on(1)
     chip_sum(3)
     pass_on(2)
+    a_first_hop()
     relay(0)
-    a_first_hop()
     relay(1)
     over_y(0)
     relay(2)
@@ -489,6 +490,7 @@
         vm((2, 16, PH), BF16),
         vm((2, 16, PC), BF16),
         vm((16, D), F32),
+        vm((HD, 512), F32),
         dma((3,)),
         dma((1,)),
         dma((7,)),

time: 67.4 us -> 67.9 us (level)
  no operation moved by 1% of the time
where the time goes in v5:
time: 67.9 us; the launch traced here: 67.8 us
  Pallas kernels  67.2 us (99%)
    pallas_call x1, Pallas kernels, per_device(): pl.pallas_call(kernel, out_shape=(jax.ShapeDtypeStruct((16, D), F32), jax...  64.9 us
    pallas_call x1, Pallas kernels, per_device(): pl.pallas_call(finish_kernel, out_shape=(jax.ShapeDtypeStruct((16, D), F3...  2.26 us

profile of v5, /device:TPU:1, one launch (start us, length us, event | category | flops | bytes accessed | tf_op | source)
XLA Modules:
  0.0 67.8 jit_solution(4393844197698388365)
XLA Ops:
  0.6 64.9 %shard_map.50 = (f32[16,8192]{1,0:T(8,128)}, bf16[4,128,128]{2,1,0:T(8,128)(2,1)}, bf16[4,2,128,128]{3,2,1,0:T(8,128)(2,1)}) custom-call(bf16[1536,128]{1,0:T(8,128)(2,1)} %bitcast.6, bf16[16,8192]{1,0:T(8,128)(2,1)} %go.1, bf16[512,8192]{1,0:T(8,128)(2,1)} %wo.1), custom_call_target="tpu_custom_call" | custom-call | tf_op jit(solution)/shard_map/pallas_call | solution.py:506
  65.5 2.3 %shard_map.51 = (f32[16,8192]{1,0:T(8,128)}, f32[1536,128]{1,0:T(8,128)}) custom-call(f32[16,8192]{1,0:T(8,128)} %get-tuple-element.7.mixed_in, bf16[4,128,128]{2,1,0:T(8,128)(2,1)} %get-tuple-element.8.dq, bf16[4,2,128,128]{3,2,1,0:T(8,128)(2,1)} %get-tuple-element.9.dkv), custom_call_target="tpu_custom_call" | custom-call | tf_op jit(solution)/shard_map/pallas_call | solution.py:520
